TPU v7x, 512 devices: a whole 4x4x16 slice. The times are simulated.
512 devices in a mesh: feat: 32 (over x, y, core), dp: 16 (over z).
Axes of the slice: x: 4, y: 4, z: 16, core: 2. Of those that a mesh axis runs over, the one named last changes fastest.
Arguments:
- feature_table: bfloat16 [65536, 256], P('feat'), may hold values from -6 to 6
- row_state: float32 [65536], P('feat'), may hold values from 0.01 to 1
- rel_diag: bfloat16 [4096, 256], replicated, may hold values from -103 to 103
- slot_rows: int32 [512, 32, 128], P(('feat', 'dp')), may hold values from 0 to 2047
- slot_counts: int32 [512, 32], P(('feat', 'dp')), may hold values from 1 to 128, as said below
- head_bags: int32 [131072, 16], P(('feat', 'dp')), may hold values from 0 to 4095, as said below
- tail_bags: int32 [131072, 16], P(('feat', 'dp')), may hold values from 0 to 4095, as said below
- negative_bags: int32 [8192, 16], P(('feat', 'dp')), may hold values from 0 to 4095, as said below
- relation_ids: int32 [131072], P(('feat', 'dp')), may hold values from 0 to 4095
Outputs:
- triple_loss: float32 [131072], P(('feat', 'dp'))
- new_table: bfloat16 [65536, 256], P('feat')
- new_state: float32 [65536], P('feat')
Inputs may be any that keep to these rules, and one draw needn't show every extreme that they name: `slot_counts`: for every device some owner has exactly 128 live slots. `head_bags`: each entry o * 128 + c names a live slot of its device: c < slot_counts[d, o]. `tail_bags`: each entry o * 128 + c names a live slot of its device: c < slot_counts[d, o]. `negative_bags`: each entry o * 128 + c names a live slot of its device: c < slot_counts[d, o].
All inputs are finite; a program needn't handle non-finite values.
Results may differ from a plain program's by a relative error of at most 0.007.
Values may be sent and summed in bfloat16 or wider, within the bound.
No kernel may reach another device: no remote copies, remote signals or barrier semaphores. Data moves between devices by JAX's collectives and lax.ppermute only.
A program may use at most 64 MiB of HBM per device.

v0:
```python
import jax
import jax.numpy as jnp
from jax import lax
from jax.sharding import PartitionSpec as P

score_scale = 4.0
learn_rate = 0.1


def adagrad(table_part, state_part, gradient):
    fresh_state = state_part + jnp.mean(gradient * gradient, axis=1)
    updated = (
        table_part.astype(jnp.float32) - learn_rate * gradient / jnp.sqrt(fresh_state)[:, None]
    )
    return (updated.astype(jnp.bfloat16), fresh_state)


def on_device(
    feature_table,
    row_state,
    rel_diag,
    slot_rows,
    slot_counts,
    head_bags,
    tail_bags,
    negative_bags,
    relation_ids,
):
    n_feat = lax.axis_size("feat")
    cap = slot_rows.shape[2]
    width = feature_table.shape[1]
    local_rows = feature_table.shape[0]
    trip = head_bags.shape[0]
    slot_total = n_feat * cap
    asked = lax.all_to_all(slot_rows[0], "feat", split_axis=0, concat_axis=0, tiled=True)
    served = jnp.take(feature_table, asked.reshape(-1), axis=0).reshape(asked.shape + (width,))
    returned = lax.all_to_all(served, "feat", split_axis=0, concat_axis=0, tiled=True)
    fetched = returned
    live_mask = (
        lax.broadcasted_iota(jnp.int32, (n_feat, cap), 1) < slot_counts[0][:, None]
    ).reshape(slot_total)
    fetched = jnp.where(
        live_mask[:, None], fetched.reshape(slot_total, width), jnp.zeros((), jnp.bfloat16)
    )
    all_bags = jnp.concatenate([head_bags, tail_bags, negative_bags], axis=0)
    bag_size = all_bags.shape[1]
    pooled = jnp.sum(jnp.take(fetched, all_bags, axis=0), axis=1, dtype=jnp.float32)
    entity = (pooled / bag_size).astype(jnp.bfloat16)
    heads = entity[:trip]
    tails = entity[trip : 2 * trip]
    own_negs = entity[2 * trip :]
    negs = lax.all_gather(own_negs, "feat", axis=0, tiled=True)
    rel_pick = (
        relation_ids[:, None] == lax.broadcasted_iota(jnp.int32, (trip, rel_diag.shape[0]), 1)
    ).astype(jnp.bfloat16)
    scaling = jnp.dot(rel_pick, rel_diag, preferred_element_type=jnp.float32)
    tails_f = tails.astype(jnp.float32)
    query = (heads.astype(jnp.float32) * scaling).astype(jnp.bfloat16)
    query_f = query.astype(jnp.float32)
    positive = score_scale * jnp.sum(query_f * tails_f, axis=1)
    negative_score = score_scale * jnp.einsum(
        "td,nd->tn", query, negs, preferred_element_type=jnp.float32
    )
    highest = jnp.maximum(jnp.max(negative_score, axis=1), positive)
    total = jnp.exp(positive - highest) + jnp.sum(
        jnp.exp(negative_score - highest[:, None]), axis=1
    )
    log_total = highest + jnp.log(total)
    triple_loss = log_total - positive
    p_pos = jnp.exp(positive - log_total)
    p_neg = jnp.exp(negative_score - log_total[:, None]).astype(jnp.bfloat16)
    grad_query = score_scale * (
        (p_pos - 1.0)[:, None] * tails_f + jnp.dot(p_neg, negs, preferred_element_type=jnp.float32)
    )
    grad_head = grad_query * scaling
    grad_tail = score_scale * (p_pos - 1.0)[:, None] * query_f
    grad_negative = lax.psum_scatter(
        (
            score_scale * jnp.einsum("tn,td->nd", p_neg, query, preferred_element_type=jnp.float32)
        ).astype(jnp.bfloat16),
        "feat",
        scatter_dimension=0,
        tiled=True,
    ).astype(jnp.float32)
    entity_grad = jnp.concatenate([grad_head, grad_tail, grad_negative], axis=0) / bag_size
    slot_grad = (
        jnp.zeros((slot_total, width), jnp.float32)
        .at[all_bags]
        .add(jnp.broadcast_to(entity_grad[:, None, :], (entity_grad.shape[0], bag_size, width)))
    )
    slot_grad = (
        jnp.where(live_mask[:, None], slot_grad, jnp.zeros((), jnp.float32))
        .astype(jnp.bfloat16)
        .reshape(n_feat, cap, width)
    )
    owner_grads = lax.all_to_all(slot_grad, "feat", split_axis=0, concat_axis=0, tiled=True)
    partial_value = jax.ops.segment_sum(
        owner_grads.reshape(slot_total, width).astype(jnp.float32),
        asked.reshape(-1),
        num_segments=local_rows,
    )
    whole = lax.psum(partial_value.astype(jnp.bfloat16), "dp").astype(jnp.float32)
    new_table, new_state = adagrad(feature_table, row_state, whole)
    return (triple_loss, new_table, new_state)


def solution(mesh):
    in_specs = (
        P("feat", None),
        P("feat"),
        P(),
        P(("feat", "dp"), None, None),
        P(("feat", "dp"), None),
        P(("feat", "dp"), None),
        P(("feat", "dp"), None),
        P(("feat", "dp"), None),
        P(("feat", "dp")),
    )
    out_specs = (P(("feat", "dp")), P("feat", None), P("feat"))
    return jax.shard_map(
        on_device, mesh=mesh, in_specs=in_specs, out_specs=out_specs, check_vma=False
    )
```

profile of v0, /device:TPU:2, one launch (start us, length us, event | category | flops | bytes accessed | tf_op | source)
XLA Modules:
  0.0 496.0 jit_solution(13791528045355781160)
XLA Ops:
  7.2 0.0 copy-start
  7.2 15.7 %all_to_all.19 = s32[32,1,128]{2,1,0:T(1,128)S(1)} all-to-all(s32[32,1,128]{2,1,0:T(1,128)} %bitcast.38), channel_id=1, replica_groups=mesh['feat'=32,'dp'=16] {'feat'}, dimensions={0} | all-to-all | bytes 32768 | tf_op jit(solution)/shard_map/all_to_all | solution.py:35
  23.0 17.2 %gather_fusion = bf16[4096,256]{1,0:T(8,128)(2,1)} fusion(bf16[2048,256]{1,0:T(8,128)(2,1)} %param.9, s32[4096]{0:T(1024)S(1)} %broadcast_clamp_fusion), kind=kCustom, calls=%fused_computation | custom fusion | bytes 4210688 | tf_op jit(solution)/shard_map/jit(_take)/gather | solution.py:36
  40.2 2.9 broadcast_select_fusion
  43.1 0.0 copy-start.4
  43.1 0.0 copy-start.5
  43.1 0.0 copy-start.14
  43.1 5.9 %all-to-all-start.1 = ((bf16[32,128,256]{2,1,0:T(8,128)(2,1)}), bf16[32,128,256]{2,1,0:T(8,128)(2,1)}, u32[]{:S(2)}, u32[]{:S(2)}) async-start(bf16[32,128,256]{2,1,0:T(8,128)(2,1)} %broadcast_select_fusion), calls=%async_computation.1 | async-start | bytes 4194304 | tf_op jit(solution)/shard_map/all_to_all | solution.py:37
  49.0 0.0 reduce-scatter.2.cloned.1.call-start
  49.1 0.0 copy-done.8
  49.1 0.1 copy.19
  49.2 0.1 copy.21
  49.2 0.0 copy-done.4
  49.2 0.0 copy-done.5
  49.3 0.2 copy.20
  49.5 0.1 copy.22
  49.6 0.1 reshape.288
  49.7 0.0 copy-start.3
  49.8 0.0 copy-done.14
  49.8 0.1 fusion.15
  49.8 0.0 copy-start.6
  49.9 25.2 %all-to-all-done.1 = bf16[32,128,256]{2,1,0:T(8,128)(2,1)} async-done(((bf16[32,128,256]{2,1,0:T(8,128)(2,1)}), bf16[32,128,256]{2,1,0:T(8,128)(2,1)}, u32[]{:S(2)}, u32[]{:S(2)}) %all-to-all-start.1) | async-done | bytes 2097184 | tf_op jit(solution)/shard_map/all_to_all | solution.py:37
  75.0 2.9 bitcast_select_fusion
  78.0 0.0 copy-done.3
  78.0 0.0 copy-done.6
  78.0 21.8 %gather_fusion.1 = bf16[8448,256]{1,0:T(8,128)(2,1)} fusion(bf16[4096,256]{1,0:T(8,128)(2,1)} %bitcast_select_fusion, s32[9216]{0:T(1024)S(1)} %pad_clamp_fusion), kind=kCustom, calls=%fused_computation.1 | custom fusion | bytes 8684544 | tf_op jit(solution)/shard_map/jit(_take)/gather | solution.py:47
  99.7 0.0 copy-start.15
  99.7 7.0 %convert_reduce_fusion = f32[528,256]{1,0:T(8,128)S(1)} fusion(bf16[528,16,256]{2,1,0:T(8,128)(2,1)} %bitcast.27, pred[528,16]{1,0:T(8,128)(4,1)S(1)} %copy.20), kind=kLoop, calls=%fused_computation.4 | loop fusion | flops 6352896 | bytes 4874496 | tf_op jit(solution)/shard_map/reduce_sum | solution.py:47
  106.8 0.0 copy-start.2
  106.8 25.0 %all_gather.3 = bf16[512,256]{1,0:T(8,128)(2,1)S(1)} all-gather(bf16[16,256]{1,0:T(8,128)(2,1)S(1)} %slice.17), channel_id=1, replica_groups=mesh['feat'=32,'dp'=16] {'feat'}, dimensions={0}, use_global_device_ids=true | all-gather | bytes 270336 | tf_op jit(solution)/shard_map/all_gather | solution.py:52
  131.8 0.0 copy-done
  131.8 0.0 copy-done.15
  131.8 1.5 fusion.14
  133.3 0.0 copy-done.2
  133.3 0.0 copy-start.11
  133.3 0.3 fusion.19
  133.6 0.2 exponential_reduce_fusion
  133.9 0.6 broadcast_multiply_fusion
  134.5 1.1 fusion.10
  135.5 0.0 reduce-scatter.2.cloned.1.call-update
  135.6 0.0 all-reduce.2.cloned.1.call-start
  135.6 0.0 copy-done.11
  135.6 0.0 copy-done.9
  135.6 0.1 convert_multiply_fusion.4
  135.7 1.3 fusion.12
  137.0 98.8 %reduce-scatter.2.cloned.1.call-done = bf16[16,256]{1,0:T(8,128)(2,1)} async-done(((bf16[512,256]{1,0:T(8,128)(2,1)}), bf16[16,256]{1,0:T(8,128)(2,1)}) %reduce-scatter.2.cloned.1.call-update) | async-done | bytes 8208 | tf_op jit(solution)/shard_map/reduce_scatter | solution.py:77
  235.9 0.7 convert_element_type.58
  236.6 4.0 broadcast_in_dim.67
  240.6 45.2 %scatter_custom_fusion = f32[4096,256]{1,0:T(8,128)} fusion(s32[8448]{0:T(1024)} %copy-done.3, f32[8448,256]{1,0:T(8,128)} %bitcast.28, f32[]{:T(128)} %constant.29.clone.1), kind=kCustom, calls=%fused_computation.17 | custom fusion | flops 2162688 | bytes 4194816 | tf_op jit(solution)/shard_map/scatter-add | solution.py:89
  285.8 0.0 copy-done.7
  285.8 2.6 select_convert_fusion
  288.4 31.4 %all_to_all.20 = bf16[32,128,256]{2,1,0:T(8,128)(2,1)} all-to-all(bf16[32,128,256]{2,1,0:T(8,128)(2,1)S(1)} %bitcast.30), channel_id=1, replica_groups=mesh['feat'=32,'dp'=16] {'feat'}, dimensions={0} | all-to-all | bytes 4194304 | tf_op jit(solution)/shard_map/all_to_all | solution.py:96
  319.9 22.3 %scatter_custom_fusion.1 = f32[2048,256]{1,0:T(8,128)} fusion(s32[4096]{0:T(1024)S(1)} %bitcast.33, bf16[4096,256]{1,0:T(8,128)(2,1)} %bitcast.29, f32[]{:T(128)} %constant.29.clone.1), kind=kCustom, calls=%fused_computation.5 | custom fusion | flops 2097152 | bytes 4194308 | tf_op jit(solution)/shard_map/scatter-add | solution.py:97
  342.1 2.8 convert_element_type.62
  344.9 0.0 all-reduce.2.cloned.1.call-update
  344.9 0.0 copy-done.10
  344.9 0.0 copy-done.12
  344.9 0.6 fusion.16
  345.5 138.8 %all-reduce.2.cloned.1.call-done = bf16[2048,256]{1,0:T(8,128)(2,1)} async-done(((bf16[2048,256]{1,0:T(8,128)(2,1)}), bf16[2048,256]{1,0:T(8,128)(2,1)}) %all-reduce.2.cloned.1.call-update) | async-done | bytes 1048592 | tf_op jit(solution)/shard_map/psum | solution.py:102
  484.3 1.6 fusion.6
  485.8 0.0 copy-done.13
  485.8 0.6 fusion.18
  486.4 0.0 copy-done.1
  486.4 2.7 fusion.5
  (17 shorter events, 0.2 us)
Async XLA Ops:
  7.2 124.7 %copy-start = (bf16[4096,256]{1,0:T(8,128)(2,1)S(1)}, bf16[4096,256]{1,0:T(8,128)(2,1)}, u32[]{:S(2)}) copy-start(bf16[4096,256]{1,0:T(8,128)(2,1)} %param.11) | copy-start | bytes 6291460
  43.1 6.0 %copy-start.8 = (s32[16,16]{1,0:T(8,128)S(1)}, s32[16,16]{1,0:T(8,128)}, u32[]{:S(2)}) copy-start(s32[16,16]{1,0:T(8,128)} %param.16) | copy-start | bytes 3076
  43.1 6.2 %copy-start.4 = (s32[256,16]{0,1:T(8,128)S(1)}, s32[256,16]{0,1:T(8,128)}, u32[]{:S(2)}) copy-start(s32[256,16]{0,1:T(8,128)} %param.15) | copy-start | bytes 49156
  43.1 6.2 %copy-start.5 = (s32[256,16]{0,1:T(8,128)S(1)}, s32[256,16]{0,1:T(8,128)}, u32[]{:S(2)}) copy-start(s32[256,16]{0,1:T(8,128)} %param.14) | copy-start | bytes 49156
  43.1 6.7 %copy-start.14 = (s32[1,32]{1,0:T(1,128)S(1)}, s32[1,32]{1,0:T(1,128)}, u32[]{:S(2)}) copy-start(s32[1,32]{1,0:T(1,128)} %param.13) | copy-start | bytes 388
  43.1 31.9 %all-to-all-start.1 = ((bf16[32,128,256]{2,1,0:T(8,128)(2,1)}), bf16[32,128,256]{2,1,0:T(8,128)(2,1)}, u32[]{:S(2)}, u32[]{:S(2)}) async-start(bf16[32,128,256]{2,1,0:T(8,128)(2,1)} %broadcast_select_fusion), calls=%async_computation.1 | async-start | bytes 4194304 | tf_op jit(solution)/shard_map/all_to_all | solution.py:37
  49.0 186.8 %reduce-scatter.2.cloned.1.call-start = ((), (), s32[]{:S(2)}) async-start(), calls=%async_computation.4 | async-start | bytes 270336 | tf_op jit(solution)/shard_map/reduce_scatter | solution.py:77
  49.7 28.2 %copy-start.3 = (s32[8448]{0:T(1024)}, s32[8448]{0:T(1024)S(1)}, u32[]{:S(2)}) copy-start(s32[8448]{0:T(1024)S(1)} %reshape.288) | copy-start | bytes 101380
  49.8 28.1 %copy-start.6 = (pred[4096]{0:T(1024)(128)(4,1)}, pred[4096]{0:T(1024)(128)(4,1)S(1)}, u32[]{:S(2)}) copy-start(pred[4096]{0:T(1024)(128)(4,1)S(1)} %fusion.15) | copy-start | bytes 12292
  99.7 32.1 %copy-start.15 = (s32[256]{0:T(256)S(1)}, s32[256]{0:T(256)}, u32[]{:S(2)}) copy-start(s32[256]{0:T(256)} %param.17) | copy-start | bytes 3076
  106.8 26.5 %copy-start.2 = (bf16[528,256]{1,0:T(8,128)(2,1)}, bf16[528,256]{1,0:T(8,128)(2,1)S(1)}, u32[]{:S(2)}) copy-start(bf16[528,256]{1,0:T(8,128)(2,1)S(1)} %multiply_convert_fusion) | copy-start | bytes 811012
  133.3 2.3 copy-start.11
  134.5 1.2 copy-start.9
  135.6 348.7 %all-reduce.2.cloned.1.call-start = ((), (), s32[]{:S(2)}) async-start(), calls=%async_computation.5 | async-start | bytes 2097152 | tf_op jit(solution)/shard_map/psum | solution.py:102
  240.6 45.2 %copy-start.7 = (pred[4096]{0:T(1024)(128)(4,1)S(1)}, pred[4096]{0:T(1024)(128)(4,1)}, u32[]{:S(2)}) copy-start(pred[4096]{0:T(1024)(128)(4,1)} %copy-done.6) | copy-start | bytes 12292
  342.1 2.8 copy-start.10
  342.1 2.8 copy-start.12
  342.1 143.7 %copy-start.13 = (f32[2048]{0:T(1024)S(1)}, f32[2048]{0:T(1024)}, u32[]{:S(2)}) copy-start(f32[2048]{0:T(1024)} %param.10) | copy-start | bytes 24580
  342.1 144.3 %copy-start.1 = (bf16[2048,256]{1,0:T(8,128)(2,1)S(1)}, bf16[2048,256]{1,0:T(8,128)(2,1)}, u32[]{:S(2)}) copy-start(bf16[2048,256]{1,0:T(8,128)(2,1)} %param.9) | copy-start | bytes 3145732
Sparse Core Ops, SparseCore 0:
  135.7 100.1 reduce-scatter.1
  345.0 139.1 all-reduce.1
where the time goes:
time: 497 us; the launch traced here: 496 us
  waiting for transfers between devices  263 us (53%)
  other arithmetic  92.9 us (19%)
  blocking collectives  72.2 us (15%)
  local copies, waits for them, and re-layouts  43.6 us (9%)
  between operations  14.3 us (3%)
  starting transfers between devices  6.02 us (1%)
    psum x1, waiting for transfers between devices, on_device(): lax.psum(partial_value.astype(jnp.bfloat16), 'dp').astype(jnp.float32)  139 us
    reduce_scatter x1, waiting for transfers between devices, on_device(): lax.psum_scatter((score_scale * jnp.einsum('tn,td->nd', p_neg, query, pre...  98.8 us
    scatter-add x1, other arithmetic, on_device(): slot_grad = jnp.zeros((slot_total, width), jnp.float32).at[all_bags].add(...  45.2 us
    all_to_all x1, blocking collectives, on_device(): lax.all_to_all(slot_grad, 'feat', split_axis=0, concat_axis=0, tiled=True)  31.4 us
    all_to_all x1, waiting for transfers between devices, on_device(): lax.all_to_all(served, 'feat', split_axis=0, concat_axis=0, tiled=True)  25.2 us
    all_gather x1, blocking collectives, on_device(): negs = lax.all_gather(own_negs, 'feat', axis=0, tiled=True)  25 us
    scatter-add x1, other arithmetic, on_device(): jax.ops.segment_sum(owner_grads.reshape(slot_total, width).astype(jnp.flo...  22.3 us
    gather x1, local copies, waits for them, and re-layouts, on_device(): jnp.take(fetched, all_bags, axis=0)  21.8 us
  transfers between devices with their start and end apart: 3, of which 3 were waited for; matrix products, arithmetic and copies ran while one was open for 1% of the time, Pallas kernels for 0%

commit v1 on v0

--- a/solution.py
+++ b/solution.py
@@ -99,7 +99,9 @@
         asked.reshape(-1),
         num_segments=local_rows,
     )
-    whole = lax.psum(partial_value.astype(jnp.bfloat16), "dp").astype(jnp.float32)
+    whole = jnp.sum(lax.all_gather(partial_value.astype(jnp.bfloat16), "dp"), axis=0).astype(
+        jnp.float32
+    )
     new_table, new_state = adagrad(feature_table, row_state, whole)
     return (triple_loss, new_table, new_state)
 

time: 497 us -> 559 us (1.12)
  the two profiles are of different devices: /device:TPU:2 before, /device:TPU:1 now
where the time goes in v1:
time: 559 us; the launch traced here: 558 us
  waiting for transfers between devices  312 us (56%)
  other arithmetic  103 us (18%)
  blocking collectives  76.4 us (14%)
  local copies, waits for them, and re-layouts  43.6 us (8%)
  between operations  14.3 us (3%)
    all_gather x1, waiting for transfers between devices, on_device(): lax.all_gather(partial_value.astype(jnp.bfloat16), 'dp')  188 us
    reduce_scatter x1, waiting for transfers between devices, on_device(): lax.psum_scatter((score_scale * jnp.einsum('tn,td->nd', p_neg, query, pre...  96.4 us
    scatter-add x1, other arithmetic, on_device(): slot_grad = jnp.zeros((slot_total, width), jnp.float32).at[all_bags].add(...  45.2 us
    all_to_all x1, blocking collectives, on_device(): lax.all_to_all(slot_grad, 'feat', split_axis=0, concat_axis=0, tiled=True)  35.7 us
    all_to_all x1, waiting for transfers between devices, on_device(): lax.all_to_all(served, 'feat', split_axis=0, concat_axis=0, tiled=True)  27.6 us
    all_gather x1, blocking collectives, on_device(): negs = lax.all_gather(own_negs, 'feat', axis=0, tiled=True)  23.2 us
    scatter-add x1, other arithmetic, on_device(): jax.ops.segment_sum(owner_grads.reshape(slot_total, width).astype(jnp.flo...  22.3 us
    gather x1, local copies, waits for them, and re-layouts, on_device(): jnp.take(fetched, all_bags, axis=0)  21.8 us
  transfers between devices with their start and end apart: 3, of which 3 were waited for; matrix products, arithmetic and copies ran while one was open for 0% of the time, Pallas kernels for 0%

profile of v1, /device:TPU:1, one launch (start us, length us, event | category | flops | bytes accessed | tf_op | source)
XLA Modules:
  0.0 558.0 jit_solution(245534236201397288)
XLA Ops:
  7.2 0.0 copy-start
  7.2 17.5 %all_to_all.19 = s32[32,1,128]{2,1,0:T(1,128)S(1)} all-to-all(s32[32,1,128]{2,1,0:T(1,128)} %bitcast.40), channel_id=1, replica_groups=mesh['feat'=32,'dp'=16] {'feat'}, dimensions={0} | all-to-all | bytes 32768 | tf_op jit(solution)/shard_map/all_to_all | solution.py:35
  24.7 17.2 %gather_fusion = bf16[4096,256]{1,0:T(8,128)(2,1)} fusion(bf16[2048,256]{1,0:T(8,128)(2,1)} %param.9, s32[4096]{0:T(1024)S(1)} %broadcast_clamp_fusion), kind=kCustom, calls=%fused_computation | custom fusion | bytes 4210688 | tf_op jit(solution)/shard_map/jit(_take)/gather | solution.py:36
  41.9 2.9 broadcast_select_fusion
  44.8 0.0 copy-start.8
  44.8 0.0 copy-start.5
  44.8 0.0 copy-start.14
  44.8 5.1 all-to-all-start.1
  50.0 0.0 reduce-scatter.2.cloned.1.call-start
  50.0 0.0 copy-done.8
  50.0 0.1 copy.23
  50.1 0.1 copy.25
  50.2 0.0 copy-done.4
  50.2 0.0 copy-done.5
  50.2 0.2 copy.24
  50.4 0.1 copy.26
  50.5 0.1 reshape.288
  50.7 0.0 copy-start.3
  50.7 0.0 copy-done.14
  50.7 0.1 fusion.15
  50.8 0.0 copy-start.6
  50.8 27.6 %all-to-all-done.1 = bf16[32,128,256]{2,1,0:T(8,128)(2,1)} async-done(((bf16[32,128,256]{2,1,0:T(8,128)(2,1)}), bf16[32,128,256]{2,1,0:T(8,128)(2,1)}, u32[]{:S(2)}, u32[]{:S(2)}) %all-to-all-start.1) | async-done | bytes 2097184 | tf_op jit(solution)/shard_map/all_to_all | solution.py:37
  78.4 2.9 bitcast_select_fusion
  81.3 0.0 copy-done.3
  81.3 0.0 copy-done.6
  81.3 21.8 %gather_fusion.1 = bf16[8448,256]{1,0:T(8,128)(2,1)} fusion(bf16[4096,256]{1,0:T(8,128)(2,1)} %bitcast_select_fusion, s32[9216]{0:T(1024)S(1)} %pad_clamp_fusion), kind=kCustom, calls=%fused_computation.1 | custom fusion | bytes 8684544 | tf_op jit(solution)/shard_map/jit(_take)/gather | solution.py:47
  103.1 0.0 copy-start.15
  103.1 7.0 %convert_reduce_fusion = f32[528,256]{1,0:T(8,128)S(1)} fusion(bf16[528,16,256]{2,1,0:T(8,128)(2,1)} %bitcast.28, pred[528,16]{1,0:T(8,128)(4,1)S(1)} %copy.24), kind=kLoop, calls=%fused_computation.4 | loop fusion | flops 6352896 | bytes 4874496 | tf_op jit(solution)/shard_map/reduce_sum | solution.py:47
  110.2 0.0 copy-start.2
  110.2 23.2 %all_gather.9 = bf16[512,256]{1,0:T(8,128)(2,1)S(1)} all-gather(bf16[16,256]{1,0:T(8,128)(2,1)S(1)} %slice.17), channel_id=1, replica_groups=mesh['feat'=32,'dp'=16] {'feat'}, dimensions={0}, use_global_device_ids=true | all-gather | bytes 270336 | tf_op jit(solution)/shard_map/all_gather | solution.py:52
  133.4 0.0 copy-done
  133.4 0.0 copy-done.15
  133.4 1.5 fusion.14
  134.8 0.0 copy-done.2
  134.8 0.3 fusion.19
  135.2 0.2 exponential_reduce_fusion
  135.4 0.6 broadcast_multiply_fusion
  136.0 1.1 fusion.10
  137.1 0.0 reduce-scatter.2.cloned.1.call-update
  137.1 0.0 all-gather.3.cloned.1.call-start
  137.2 0.0 copy-done.11
  137.2 0.0 copy-done.9
  137.2 0.1 convert_multiply_fusion.4
  137.3 1.3 fusion.12
  138.6 96.4 %reduce-scatter.2.cloned.1.call-done = bf16[16,256]{1,0:T(8,128)(2,1)} async-done(((bf16[512,256]{1,0:T(8,128)(2,1)}), bf16[16,256]{1,0:T(8,128)(2,1)}) %reduce-scatter.2.cloned.1.call-update) | async-done | bytes 8208 | tf_op jit(solution)/shard_map/reduce_scatter | solution.py:77
  235.0 0.7 convert_element_type.60
  235.8 4.0 broadcast_in_dim.67
  239.8 45.2 %scatter_custom_fusion = f32[4096,256]{1,0:T(8,128)} fusion(s32[8448]{0:T(1024)} %copy-done.3, f32[8448,256]{1,0:T(8,128)} %bitcast.30, f32[]{:T(128)} %constant.30.clone.1), kind=kCustom, calls=%fused_computation.17 | custom fusion | flops 2162688 | bytes 4194816 | tf_op jit(solution)/shard_map/scatter-add | solution.py:89
  285.0 0.0 copy-done.7
  285.0 2.6 select_convert_fusion
  287.6 35.7 %all_to_all.20 = bf16[32,128,256]{2,1,0:T(8,128)(2,1)} all-to-all(bf16[32,128,256]{2,1,0:T(8,128)(2,1)S(1)} %bitcast.32), channel_id=1, replica_groups=mesh['feat'=32,'dp'=16] {'feat'}, dimensions={0} | all-to-all | bytes 4194304 | tf_op jit(solution)/shard_map/all_to_all | solution.py:96
  323.3 22.3 %scatter_custom_fusion.1 = f32[2048,256]{1,0:T(8,128)} fusion(s32[4096]{0:T(1024)S(1)} %bitcast.35, bf16[4096,256]{1,0:T(8,128)(2,1)} %bitcast.31, f32[]{:T(128)} %constant.30.clone.1), kind=kCustom, calls=%fused_computation.5 | custom fusion | flops 2097152 | bytes 4194308 | tf_op jit(solution)/shard_map/scatter-add | solution.py:97
  345.6 2.7 convert_element_type.64
  348.2 0.0 all-gather.3.cloned.1.call-update
  348.3 0.0 copy-done.10
  348.3 0.0 copy-done.12
  348.3 0.6 fusion.16
  348.8 187.5 %all-gather.3.cloned.1.call-done = bf16[32768,256]{1,0:T(8,128)(2,1)} async-done(((bf16[2048,256]{1,0:T(8,128)(2,1)}), bf16[32768,256]{1,0:T(8,128)(2,1)}) %all-gather.3.cloned.1.call-update) | async-done | bytes 16777232 | tf_op jit(solution)/shard_map/all_gather | solution.py:102
  536.4 9.9 %reduce_sum.51 = bf16[2048,256]{1,0:T(8,128)(2,1)} reduce(bf16[16,2048,256]{2,1,0:T(8,128)(2,1)} %bitcast.29, bf16[]{:T(256)} %constant.29.clone.1), dimensions={0}, to_apply=%region_7.8 | reduce | flops 7864320 | bytes 17825794 | tf_op jit(solution)/shard_map/reduce_sum | solution.py:102
  546.3 1.6 fusion.6
  547.9 0.0 copy-done.13
  547.9 0.6 fusion.18
  548.5 0.0 copy-done.1
  548.5 2.7 fusion.5
  (18 shorter events, 0.2 us)
Async XLA Ops:
  7.2 126.2 %copy-start = (bf16[4096,256]{1,0:T(8,128)(2,1)S(1)}, bf16[4096,256]{1,0:T(8,128)(2,1)}, u32[]{:S(2)}) copy-start(bf16[4096,256]{1,0:T(8,128)(2,1)} %param.11) | copy-start | bytes 6291460
  44.8 5.2 copy-start.8
  44.8 5.4 copy-start.4
  44.8 5.4 copy-start.5
  44.8 5.9 %copy-start.14 = (s32[1,32]{1,0:T(1,128)S(1)}, s32[1,32]{1,0:T(1,128)}, u32[]{:S(2)}) copy-start(s32[1,32]{1,0:T(1,128)} %param.13) | copy-start | bytes 388
  44.8 33.6 %all-to-all-start.1 = ((bf16[32,128,256]{2,1,0:T(8,128)(2,1)}), bf16[32,128,256]{2,1,0:T(8,128)(2,1)}, u32[]{:S(2)}, u32[]{:S(2)}) async-start(bf16[32,128,256]{2,1,0:T(8,128)(2,1)} %broadcast_select_fusion), calls=%async_computation.1 | async-start | bytes 4194304 | tf_op jit(solution)/shard_map/all_to_all | solution.py:37
  50.0 185.1 %reduce-scatter.2.cloned.1.call-start = ((), (), s32[]{:S(2)}) async-start(), calls=%async_computation.4 | async-start | bytes 270336 | tf_op jit(solution)/shard_map/reduce_scatter | solution.py:77
  50.7 30.6 %copy-start.3 = (s32[8448]{0:T(1024)}, s32[8448]{0:T(1024)S(1)}, u32[]{:S(2)}) copy-start(s32[8448]{0:T(1024)S(1)} %reshape.288) | copy-start | bytes 101380
  50.8 30.6 %copy-start.6 = (pred[4096]{0:T(1024)(128)(4,1)}, pred[4096]{0:T(1024)(128)(4,1)S(1)}, u32[]{:S(2)}) copy-start(pred[4096]{0:T(1024)(128)(4,1)S(1)} %fusion.15) | copy-start | bytes 12292
  103.1 30.3 %copy-start.15 = (s32[256]{0:T(256)S(1)}, s32[256]{0:T(256)}, u32[]{:S(2)}) copy-start(s32[256]{0:T(256)} %param.17) | copy-start | bytes 3076
  110.2 24.7 %copy-start.2 = (bf16[528,256]{1,0:T(8,128)(2,1)}, bf16[528,256]{1,0:T(8,128)(2,1)S(1)}, u32[]{:S(2)}) copy-start(bf16[528,256]{1,0:T(8,128)(2,1)S(1)} %multiply_convert_fusion) | copy-start | bytes 811012
  134.8 2.3 copy-start.11
  136.0 1.2 copy-start.9
  137.1 399.2 %all-gather.3.cloned.1.call-start = ((), (), s32[]{:S(2)}) async-start(), calls=%async_computation.5 | async-start | bytes 17825792 | tf_op jit(solution)/shard_map/all_gather | solution.py:102
  239.8 45.2 %copy-start.7 = (pred[4096]{0:T(1024)(128)(4,1)S(1)}, pred[4096]{0:T(1024)(128)(4,1)}, u32[]{:S(2)}) copy-start(pred[4096]{0:T(1024)(128)(4,1)} %copy-done.6) | copy-start | bytes 12292
  345.6 2.7 copy-start.10
  345.6 2.7 copy-start.12
  536.4 11.5 %copy-start.13 = (f32[2048]{0:T(1024)S(1)}, f32[2048]{0:T(1024)}, u32[]{:S(2)}) copy-start(f32[2048]{0:T(1024)} %param.10) | copy-start | bytes 24580
  536.4 12.1 %copy-start.1 = (bf16[2048,256]{1,0:T(8,128)(2,1)S(1)}, bf16[2048,256]{1,0:T(8,128)(2,1)}, u32[]{:S(2)}) copy-start(bf16[2048,256]{1,0:T(8,128)(2,1)} %param.9) | copy-start | bytes 3145732
Sparse Core Ops, SparseCore 0:
  137.2 97.7 reduce-scatter.1
  348.4 187.9 all-gather.2
